TPU v7x, 128 devices: a whole 4x4x4 slice. The times are simulated.
128 devices in a mesh: sub: 32 (over y, z, x_lo), band: 4 (over x_hi, core).
Axes of the slice: x: 4 (x_hi: 2, x_lo: 2; x = x_hi * 2 + x_lo), y: 4, z: 4, core: 2. Of those that a mesh axis runs over, the one named last changes fastest.
Arguments:
- intensity: bfloat16 [4, 16384, 8192], P(None, ('band', 'sub')), may hold values from -6 to 6
- channel_spans: int32 [16384], replicated, may hold values from 1 to 8
Outputs:
- dedispersed: float32 [4, 2048, 8192], P(None, ('band', 'sub'))
- peak_snr: float32 [4, 2048, 8192], P(None, ('band', 'sub'))
All inputs are finite; a program needn't handle non-finite values.
Results may differ from a plain program's by a relative error of at most 0.0003.
Values sent between devices are 32-bit elements; how exact they have to be, the bound alone decides.
A program may use at most 128 MiB of HBM per device.

v0:
```python
import math

import jax
import jax.numpy as jnp
from jax import lax
from jax.experimental import pallas as pl
from jax.experimental.pallas import tpu as pltpu
from jax.sharding import PartitionSpec as P

ROWS = 16
BOXES = 9
BEAMS = 4
LANES = 128
BODY = 64
PAD = 8
PITCH = PAD + BODY
TOP_PAD = 16
TOP_PITCH = TOP_PAD + BODY
COLUMNS = 1024


def rev2(v):
    return v % 2 * 2 + v // 2


def rev3(v):
    return v % 2 * 4 + v // 2 % 2 * 2 + v // 4


def shift_table(spans):
    sub, band = lax.axis_index("sub"), lax.axis_index("band")
    sums = spans.reshape(1024, 16).sum(axis=1)
    device = band * 32 + sub
    local = lax.dynamic_slice_in_dim(sums, device * 8, 8)
    totals = sums.reshape(128, 8).sum(axis=1)
    group = lax.dynamic_slice_in_dim(totals, device // 8 * 8, 8)
    block = rev3(sub % 8)
    own = block * 16 + rev2(sub // 8) * 4 + rev2(band)
    tables = []
    for widths, rows, first in (
        (local, 4, 0), (local, 8, 0), (local, 16, 0),
        (group, 4, 4 * block), (group, 8, 8 * block), (group, 16, 16 * block),
        (totals, 2, 2 * own), (totals, 4, 4 * own), (totals, 8, 8 * own), (totals, 16, 16 * own),
    ):
        grouped = widths.reshape(16 // rows, 2, -1).sum(axis=2)
        low, high = grouped[:, 0:1], grouped[:, 1:2]
        r = first + jnp.arange(rows, dtype=jnp.int32)[None, :]
        tables.append((r * low // (low + high)).reshape(-1))
    return jnp.concatenate(tables)


def kernel(
    table, x_hbm, ded_hbm, peak_hbm,
    xbuf, g, t5, t6, p7, r1, t8, t9, p10, r2, t11, t12, t13, top, ded, peak,
    in_sem, out_sem, send1, recv1, own1, send2, recv2, own2,
):
    sub, band = lax.axis_index("sub"), lax.axis_index("band")
    y, z, x_lo = sub // 8, sub // 2 % 4, sub % 2
    x_hi, core = band // 2, band % 2
    j = sub % 8
    m = band * 4 + y

    peers1 = []
    for dz in (0, 1, 3, 2):
        for dx in range(2):
            if dz or dx:
                to = (z + dz) % 4 * 2 + (x_lo + dx) % 2
                peers1.append((to, {"sub": y * 8 + to, "band": band}))
    peers2 = []
    for dy in (0, 1, 3, 2):
        for dh in range(2):
            for dc in range(2):
                if dy or dh or dc:
                    y_to = (y + dy) % 4
                    band_to = (x_hi + dh) % 2 * 2 + (core + dc) % 2
                    peers2.append((y_to, band_to, {"sub": y_to * 8 + j, "band": band_to}))

    barrier = pltpu.get_barrier_semaphore()
    for peer in peers1:
        pl.semaphore_signal(barrier, inc=1, device_id=peer[-1], device_id_type=pl.DeviceIdType.MESH)
    for peer in peers2:
        pl.semaphore_signal(barrier, inc=1, device_id=peer[-1], device_id_type=pl.DeviceIdType.MESH)

    def fetch(b):
        return pltpu.make_async_copy(x_hbm.at[b], xbuf.at[b], in_sem.at[b])

    for b in range(BEAMS):
        fetch(b).start()

    zeros = jnp.zeros((PAD, LANES), jnp.float32)
    for ref, count in ((g, 8), (t5, 16), (t6, 16), (t8, 16), (t9, 16), (t11, 16), (t12, 16)):
        for row in range(count):
            ref[pl.ds(row * PITCH, PAD), :] = zeros
    for row in range(16):
        t13[pl.ds(row * TOP_PITCH, PAD), :] = zeros
        t13[pl.ds(row * TOP_PITCH + PAD, PAD), :] = zeros

    def clear(b, _):
        for row in range(16):
            r1[b, row // 2, row % 2, 0:PAD, :] = zeros
            r2[b, row, 0:PAD, :] = zeros
        return 0

    lax.fori_loop(0, BEAMS, clear, 0)

    lane = lax.broadcasted_iota(jnp.int32, (BODY, LANES), 1)

    def moved(near, far, amount):
        return pltpu.roll(jnp.where(lane < LANES - amount, near, far), amount, 1)

    def flat(ref):
        def load(row, back):
            return ref[pl.ds(row * PITCH + PAD - back, BODY), :]
        return load

    def flat_store(ref):
        def store(row, value):
            ref[pl.ds(row * PITCH + PAD, BODY), :] = value
        return store

    def small_level(level, rows, load, store, single=False):
        for entry in range(16):
            pair, i = entry // rows, entry % rows
            if single:
                low, high = 2 * pair, 2 * pair + 1
            else:
                low = pair * rows + i // 2
                high = low + rows // 2
            amount = table[(level - 5) * 16 + entry]
            store(entry, load(low, 0) + moved(load(high, 0), load(high, 1), amount))

    def large_level(level, rows, load, store):
        for entry in range(16):
            pair, i = entry // rows, entry % rows
            low = pair * rows + i // 2
            high = low + rows // 2
            shift = table[(level - 5) * 16 + entry]
            whole, amount = shift // LANES, shift % LANES
            store(entry, load(low, 0) + moved(load(high, whole), load(high, whole + 1), amount))

    member = lax.broadcasted_iota(jnp.int32, (16, 128), 0)
    channel = lax.broadcasted_iota(jnp.int32, (16, 128), 1)
    ones = (channel // 16 == member).astype(jnp.float32).astype(jnp.bfloat16)

    def send_one(b, k):
        to, device = peers1[k]
        return pltpu.make_async_remote_copy(
            src_ref=p7.at[b, pl.ds(2 * rev3(to), 2)],
            dst_ref=r1.at[b, j, :, pl.ds(PAD, BODY), :],
            send_sem=send1.at[b, k],
            recv_sem=recv1.at[b, j],
            device_id=device,
            device_id_type=pl.DeviceIdType.MESH,
        )

    def keep_one(b):
        return pltpu.make_async_copy(
            p7.at[b, pl.ds(2 * rev3(j), 2)], r1.at[b, j, :, pl.ds(PAD, BODY), :], own1.at[b]
        )

    def send_two(b, k):
        y_to, band_to, device = peers2[k]
        return pltpu.make_async_remote_copy(
            src_ref=p10.at[b, rev2(y_to) * 4 + rev2(band_to)],
            dst_ref=r2.at[b, m, pl.ds(PAD, BODY), :],
            send_sem=send2.at[b, k],
            recv_sem=recv2.at[b, m],
            device_id=device,
            device_id_type=pl.DeviceIdType.MESH,
        )

    def keep_two(b):
        return pltpu.make_async_copy(
            p10.at[b, rev2(y) * 4 + rev2(band)], r2.at[b, m, pl.ds(PAD, BODY), :], own2.at[b]
        )

    def first(b):
        fetch(b).wait()

        def columns(c, _):
            part = jnp.dot(
                ones, xbuf[b, :, pl.ds(c * COLUMNS, COLUMNS)], preferred_element_type=jnp.float32
            )
            for k in range(COLUMNS // LANES):
                g[pl.ds(PAD + c * (COLUMNS // LANES) + k, 8, stride=PITCH), :] = part[
                    0:8, k * LANES : (k + 1) * LANES
                ]
            return 0

        lax.fori_loop(0, 8192 // COLUMNS, columns, 0)
        small_level(5, 4, flat(g), flat_store(t5), single=True)
        small_level(6, 8, flat(t5), flat_store(t6))

        def keep(row, value):
            p7[b, row] = value

        small_level(7, 16, flat(t6), keep)

    def start_one(b):
        for k in range(len(peers1)):
            send_one(b, k).start()
        keep_one(b).start()

    first(0)
    pl.semaphore_wait(barrier, len(peers1) + len(peers2))
    start_one(0)

    def step_one(b, _):
        first(b)
        start_one(b)
        return 0

    lax.fori_loop(1, BEAMS, step_one, 0)

    def step_two(b, _):
        keep_one(b).wait()
        for to, _ in peers1:
            pltpu.make_async_copy(
                r1.at[b, to, :, pl.ds(PAD, BODY), :], r1.at[b, to, :, pl.ds(PAD, BODY), :], recv1.at[b, to]
            ).wait()

        def load(row, back):
            return r1[b, row // 2, row % 2, PAD - back : PAD - back + BODY, :]

        small_level(8, 4, load, flat_store(t8))
        small_level(9, 8, flat(t8), flat_store(t9))

        def keep(row, value):
            p10[b, row] = value

        small_level(10, 16, flat(t9), keep)
        for k in range(len(peers2)):
            send_two(b, k).start()
        keep_two(b).start()
        return 0

    lax.fori_loop(0, BEAMS, step_two, 0)

    one_lane = lax.broadcasted_iota(jnp.int32, (8, LANES), 1)

    def step_three(b, _):
        keep_two(b).wait()
        for y_to, band_to, _ in peers2:
            n = band_to * 4 + y_to
            pltpu.make_async_copy(
                r2.at[b, n, pl.ds(PAD, BODY), :], r2.at[b, n, pl.ds(PAD, BODY), :], recv2.at[b, n]
            ).wait()
        for entry in range(16):
            pair = entry // 2
            shift = table[6 * 16 + entry]
            whole, amount = shift // LANES, shift % LANES
            back0 = r2[b, 2 * pair + 1, PAD : PAD + BODY, :]
            back1 = r2[b, 2 * pair + 1, PAD - 1 : PAD - 1 + BODY, :]
            back2 = r2[b, 2 * pair + 1, PAD - 2 : PAD - 2 + BODY, :]
            near = jnp.where(whole == 0, back0, back1)
            far = jnp.where(whole == 0, back1, back2)
            t11[pl.ds(entry * PITCH + PAD, BODY), :] = r2[b, 2 * pair, PAD : PAD + BODY, :] + moved(
                near, far, amount
            )
        large_level(12, 4, flat(t11), flat_store(t12))

        def store13(row, value):
            t13[pl.ds(row * TOP_PITCH + TOP_PAD, BODY), :] = value

        def load13(row, back):
            return t13[pl.ds(row * TOP_PITCH + TOP_PAD - back, BODY), :]

        large_level(13, 8, flat(t12), store13)

        def store14(row, value):
            top[pl.ds(row * BODY, BODY), :] = value * (1.0 / 128.0)

        large_level(14, 16, load13, store14)

        blank = jnp.zeros((8, LANES), jnp.float32)
        for half in range(2):

            def boxes(c, before):
                before = list(before)
                for u in range(8):
                    running = top[pl.ds(half * 8 * BODY + c * 8 + u, 8, stride=BODY), :]
                    column = pl.ds(pl.multiple_of((c * 8 + u) * LANES, LANES), LANES)
                    ded[b, half * 8 : half * 8 + 8, column] = running
                    best = running
                    for k in range(BOXES - 1):
                        width = 2**k
                        if width < LANES:
                            late = pltpu.roll(
                                jnp.where(one_lane < LANES - width, running, before[k]), width, 1
                            )
                        else:
                            late = before[k]
                        before[k] = running
                        running = running + late
                        best = jnp.maximum(best, running * (1.0 / math.sqrt(2 * width)))
                    peak[b, half * 8 : half * 8 + 8, column] = best
                return tuple(before)

            lax.fori_loop(0, BODY // 8, boxes, (blank,) * (BOXES - 1))
        pltpu.make_async_copy(ded.at[b], ded_hbm.at[b], out_sem.at[b, 0]).start()
        pltpu.make_async_copy(peak.at[b], peak_hbm.at[b], out_sem.at[b, 1]).start()
        return 0

    lax.fori_loop(0, BEAMS, step_three, 0)

    def finish(b, _):
        pltpu.make_async_copy(ded.at[b], ded_hbm.at[b], out_sem.at[b, 0]).wait()
        pltpu.make_async_copy(peak.at[b], peak_hbm.at[b], out_sem.at[b, 1]).wait()
        for k in range(len(peers1)):
            send_one(b, k).wait_send()
        for k in range(len(peers2)):
            send_two(b, k).wait_send()
        return 0

    lax.fori_loop(0, BEAMS, finish, 0)


def on_device(intensity, channel_spans):
    plane = jax.ShapeDtypeStruct((BEAMS, ROWS, 8192), jnp.float32)
    vmem = lambda *shape: pltpu.VMEM(shape, jnp.float32)
    dma = pltpu.SemaphoreType.DMA
    return pl.pallas_call(
        kernel,
        out_shape=(plane, plane),
        in_specs=[pl.BlockSpec(memory_space=pltpu.SMEM), pl.BlockSpec(memory_space=pl.ANY)],
        out_specs=(pl.BlockSpec(memory_space=pl.ANY), pl.BlockSpec(memory_space=pl.ANY)),
        scratch_shapes=[
            pltpu.VMEM((BEAMS, 128, 8192), jnp.bfloat16),
            vmem(8 * PITCH, LANES),
            vmem(16 * PITCH, LANES),
            vmem(16 * PITCH, LANES),
            vmem(BEAMS, 16, BODY, LANES),
            vmem(BEAMS, 8, 2, PITCH, LANES),
            vmem(16 * PITCH, LANES),
            vmem(16 * PITCH, LANES),
            vmem(BEAMS, 16, BODY, LANES),
            vmem(BEAMS, 16, PITCH, LANES),
            vmem(16 * PITCH, LANES),
            vmem(16 * PITCH, LANES),
            vmem(16 * TOP_PITCH, LANES),
            vmem(16 * BODY, LANES),
            vmem(BEAMS, ROWS, 8192),
            vmem(BEAMS, ROWS, 8192),
            dma((BEAMS,)),
            dma((BEAMS, 2)),
            dma((BEAMS, 7)),
            dma((BEAMS, 8)),
            dma((BEAMS,)),
            dma((BEAMS, 15)),
            dma((BEAMS, 16)),
            dma((BEAMS,)),
        ],
        compiler_params=pltpu.CompilerParams(
            collective_id=0, has_side_effects=True, vmem_limit_bytes=48 * 2**20
        ),
    )(shift_table(channel_spans), intensity)


def solution(mesh):
    return jax.shard_map(
        on_device,
        mesh=mesh,
        in_specs=(P(None, ("band", "sub"), None), P()),
        out_specs=(P(None, ("band", "sub"), None), P(None, ("band", "sub"), None)),
        check_vma=False,
    )
```

profile of v0, /device:TPU:1, one launch (start us, length us, event | category | flops | bytes accessed | tf_op | source)
XLA Modules:
  0.0 98.6 jit_solution(602752711879950433)
XLA Ops:
  0.8 1.0 %reshape.151 = s32[1024,16]{1,0:T(8,128)S(1)} reshape(s32[16384]{0:T(1024)} %param.9) | data formatting | bytes 131072 | tf_op jit(solution)/shard_map/reshape | solution.py:32
  1.9 0.2 reduce_sum.108
  2.2 0.1 reduce_sum.111
  2.4 0.6 fusion.22
  4.3 0.8 fusion.13
  5.1 0.1 reduce_sum.110
  5.2 0.2 slice_reduce_fusion.6
  5.5 0.2 and_select_fusion.5
  5.8 0.2 slice_reduce_fusion.3
  6.0 0.2 add_select_fusion.2
  6.7 0.1 reduce_sum.116
  6.8 0.6 fusion.21
  8.7 0.1 reduce_sum.121
  8.8 0.6 fusion.20
  10.7 1.3 %fusion.11 = (s32[16]{0:T(128)S(1)}, s32[16]{0:T(128)S(1)}) fusion(s32[]{:T(128)} %bitcast.13, s32[]{:T(128)} %bitcast.12, s32[]{:T(128)} %bitcast.11, s32[]{:T(128)S(6)} %mul.255, s32[]{:T(128)} %bitcast.8, s32[]{:T(128)} %bitcast.7, s32[]{:T(128)} %bitcast.6, s32[]{:T(128)S(6)} %mul.233), kind=kLoop, calls=%fused_computation.60 | loop fusion | flops 320 | bytes 160 | tf_op jit(solution)/shard_map/reshape | solution.py:48
  12.1 0.1 reduce_sum.115
  12.3 0.2 slice_reduce_fusion.2
  12.6 0.2 add_select_fusion.1
  12.9 0.1 reduce_sum.120
  13.1 0.3 slice_reduce_fusion.4
  13.3 0.2 and_select_fusion.1
  13.6 0.2 and_select_fusion.3
  14.0 0.1 reduce_sum.119
  14.1 0.2 slice_reduce_fusion.1
  14.3 0.2 add_select_fusion
  14.7 0.2 reduce_sum.118
  14.9 0.2 slice_reduce_fusion
  15.2 0.2 fusion.2
  15.5 0.2 multiply_divide_fusion
  15.8 80.1 %shard_map.41 = (f32[4,16,8192]{2,1,0:T(8,128)S(1)}, f32[4,16,8192]{2,1,0:T(8,128)S(1)}) custom-call(s32[160]{0:T(256)S(1)} %concatenate.3.table, bf16[4,128,8192]{2,1,0:T(8,128)(2,1)} %x_hbm.1), custom_call_target="tpu_custom_call" | custom-call | tf_op jit(solution)/shard_map/pallas_call | solution.py:322
  95.9 1.3 %copy.6 = f32[4,16,8192]{2,1,0:T(8,128)} copy(f32[4,16,8192]{2,1,0:T(8,128)S(1)} %get-tuple-element.39) | data formatting | bytes 4194304
  97.3 1.3 %copy.7 = f32[4,16,8192]{2,1,0:T(8,128)} copy(f32[4,16,8192]{2,1,0:T(8,128)S(1)} %get-tuple-element.40) | data formatting | bytes 4194304
  (29 shorter events, 2.0 us)
where the time goes:
time: 98.8 us; the launch traced here: 98.6 us
  Pallas kernels  80.1 us (81%)
  local copies, waits for them, and re-layouts  7.25 us (7%)
  other arithmetic  6.46 us (7%)
  between operations  4.77 us (5%)
    pallas_call x1, Pallas kernels, on_device(): pl.pallas_call(kernel, out_shape=(plane, plane), in_specs=[pl.BlockSpec(m...  80.1 us
    unnamed x2, local copies, waits for them, and re-layouts  2.64 us
    reshape x2, other arithmetic, shift_table(): tables.append((r * low // (low + high)).reshape(-1))  2.11 us

commit v1 on v0

--- a/solution.py
+++ b/solution.py
@@ -27,32 +27,55 @@
     return v % 2 * 4 + v // 2 % 2 * 2 + v // 4
 
 
-def shift_table(spans):
-    sub, band = lax.axis_index("sub"), lax.axis_index("band")
-    sums = spans.reshape(1024, 16).sum(axis=1)
-    device = band * 32 + sub
-    local = lax.dynamic_slice_in_dim(sums, device * 8, 8)
-    totals = sums.reshape(128, 8).sum(axis=1)
-    group = lax.dynamic_slice_in_dim(totals, device // 8 * 8, 8)
-    block = rev3(sub % 8)
-    own = block * 16 + rev2(sub // 8) * 4 + rev2(band)
-    tables = []
-    for widths, rows, first in (
-        (local, 4, 0), (local, 8, 0), (local, 16, 0),
-        (group, 4, 4 * block), (group, 8, 8 * block), (group, 16, 16 * block),
-        (totals, 2, 2 * own), (totals, 4, 4 * own), (totals, 8, 8 * own), (totals, 16, 16 * own),
-    ):
-        grouped = widths.reshape(16 // rows, 2, -1).sum(axis=2)
-        low, high = grouped[:, 0:1], grouped[:, 1:2]
-        r = first + jnp.arange(rows, dtype=jnp.int32)[None, :]
-        tables.append((r * low // (low + high)).reshape(-1))
-    return jnp.concatenate(tables)
+def powers(index, first):
+    value = jnp.full(index.shape, first, jnp.int32)
+    for k in range(1, 7):
+        value = jnp.where(index == k, first * 2**k, value)
+    return value
+
+
+def quotient(top, bottom):
+    guess = (top.astype(jnp.float32) / bottom.astype(jnp.float32)).astype(jnp.int32)
+    left = top - guess * bottom
+    return jnp.where(left < 0, guess - 1, jnp.where(left >= bottom, guess + 1, guess))
+
+
+def fill_tables(spans, out, device, group, block, own):
+    spread = spans[...].astype(jnp.float32)
+    totals = jnp.sum(spread, axis=1, keepdims=True)
+    entry = lax.broadcasted_iota(jnp.int32, (1, LANES), 1)
+    level = entry // 16
+    near = level < 3
+    rows = jnp.where(near, powers(level, 4), powers(level - 3, 2))
+    half = powers(level, 1)
+    start = jnp.where(near, group, 0) + entry % 16 // rows * 2 * half
+    r = rows * jnp.where(near, block, own) + entry % 16 % rows
+    place = lax.broadcasted_iota(jnp.int32, (128, LANES), 0) - start
+    low = jnp.sum(jnp.where((place >= 0) & (place < half), totals, 0.0), axis=0, keepdims=True)
+    both = jnp.sum(jnp.where((place >= 0) & (place < 2 * half), totals, 0.0), axis=0, keepdims=True)
+    low, both = low.astype(jnp.int32), jnp.maximum(both.astype(jnp.int32), 1)
+    out[0:1, :] = quotient(r * low, both)
+
+    mine = spans[pl.ds(device, 1), :].astype(jnp.float32)
+    entry = lax.broadcasted_iota(jnp.int32, (48, 1), 0)
+    level = entry // 16
+    rows = powers(level, 4)
+    half = powers(level, 16)
+    start = entry % 16 // rows * 2 * half
+    r = entry % 16 % rows
+    place = lax.broadcasted_iota(jnp.int32, (48, LANES), 1) - start
+    low = jnp.sum(jnp.where((place >= 0) & (place < half), mine, 0.0), axis=1, keepdims=True)
+    both = jnp.sum(jnp.where((place >= 0) & (place < 2 * half), mine, 0.0), axis=1, keepdims=True)
+    low, both = low.astype(jnp.int32), jnp.maximum(both.astype(jnp.int32), 1)
+    shifts = quotient(r * low, both).astype(jnp.float32)
+    diagonal = entry == lax.broadcasted_iota(jnp.int32, (48, LANES), 1)
+    out[1:2, :] = jnp.sum(jnp.where(diagonal, shifts, 0.0), axis=0, keepdims=True).astype(jnp.int32)
 
 
 def kernel(
-    table, x_hbm, ded_hbm, peak_hbm,
-    xbuf, g, t5, t6, p7, r1, t8, t9, p10, r2, t11, t12, t13, top, ded, peak,
-    in_sem, out_sem, send1, recv1, own1, send2, recv2, own2,
+    spans, x_hbm, ded, peak,
+    shifts, table, xbuf, g, t5, t6, p7, r1, t8, t9, p10, r2, t11, t12, t13, top,
+    table_sem, in_sem, send1, recv1, own1, send2, recv2, own2,
 ):
     sub, band = lax.axis_index("sub"), lax.axis_index("band")
     y, z, x_lo = sub // 8, sub // 2 % 4, sub % 2
@@ -103,6 +126,17 @@
 
     lax.fori_loop(0, BEAMS, clear, 0)
 
+    block = rev3(j)
+    fill_tables(
+        spans, shifts, band * 32 + sub, band * 32 + y * 8, block, block * 16 + rev2(y) * 4 + rev2(band)
+    )
+    to_scalar = pltpu.make_async_copy(shifts, table, table_sem)
+    to_scalar.start()
+    to_scalar.wait()
+
+    def shift_of(level, entry):
+        return table[0, (level - 8) * 16 + entry] if level >= 8 else table[1, (level - 5) * 16 + entry]
+
     lane = lax.broadcasted_iota(jnp.int32, (BODY, LANES), 1)
 
     def moved(near, far, amount):
@@ -126,7 +160,7 @@
             else:
                 low = pair * rows + i // 2
                 high = low + rows // 2
-            amount = table[(level - 5) * 16 + entry]
+            amount = shift_of(level, entry)
             store(entry, load(low, 0) + moved(load(high, 0), load(high, 1), amount))
 
     def large_level(level, rows, load, store):
@@ -134,8 +168,8 @@
             pair, i = entry // rows, entry % rows
             low = pair * rows + i // 2
             high = low + rows // 2
-            shift = table[(level - 5) * 16 + entry]
-            whole, amount = shift // LANES, shift % LANES
+            shift = shift_of(level, entry)
+            whole, amount = jnp.clip(shift // LANES, 0, 2 ** (level - 10) - 1), shift % LANES
             store(entry, load(low, 0) + moved(load(high, whole), load(high, whole + 1), amount))
 
     member = lax.broadcasted_iota(jnp.int32, (16, 128), 0)
@@ -177,17 +211,14 @@
     def first(b):
         fetch(b).wait()
 
-        def columns(c, _):
+        for c in range(8192 // COLUMNS):
             part = jnp.dot(
-                ones, xbuf[b, :, pl.ds(c * COLUMNS, COLUMNS)], preferred_element_type=jnp.float32
+                ones, xbuf[b, :, c * COLUMNS : (c + 1) * COLUMNS], preferred_element_type=jnp.float32
             )
             for k in range(COLUMNS // LANES):
                 g[pl.ds(PAD + c * (COLUMNS // LANES) + k, 8, stride=PITCH), :] = part[
                     0:8, k * LANES : (k + 1) * LANES
                 ]
-            return 0
-
-        lax.fori_loop(0, 8192 // COLUMNS, columns, 0)
         small_level(5, 4, flat(g), flat_store(t5), single=True)
         small_level(6, 8, flat(t5), flat_store(t6))
 
@@ -247,7 +278,7 @@
             ).wait()
         for entry in range(16):
             pair = entry // 2
-            shift = table[6 * 16 + entry]
+            shift = shift_of(11, entry)
             whole, amount = shift // LANES, shift % LANES
             back0 = r2[b, 2 * pair + 1, PAD : PAD + BODY, :]
             back1 = r2[b, 2 * pair + 1, PAD - 1 : PAD - 1 + BODY, :]
@@ -274,38 +305,29 @@
 
         blank = jnp.zeros((8, LANES), jnp.float32)
         for half in range(2):
-
-            def boxes(c, before):
-                before = list(before)
-                for u in range(8):
-                    running = top[pl.ds(half * 8 * BODY + c * 8 + u, 8, stride=BODY), :]
-                    column = pl.ds(pl.multiple_of((c * 8 + u) * LANES, LANES), LANES)
-                    ded[b, half * 8 : half * 8 + 8, column] = running
-                    best = running
-                    for k in range(BOXES - 1):
-                        width = 2**k
-                        if width < LANES:
-                            late = pltpu.roll(
-                                jnp.where(one_lane < LANES - width, running, before[k]), width, 1
-                            )
-                        else:
-                            late = before[k]
-                        before[k] = running
-                        running = running + late
-                        best = jnp.maximum(best, running * (1.0 / math.sqrt(2 * width)))
-                    peak[b, half * 8 : half * 8 + 8, column] = best
-                return tuple(before)
-
-            lax.fori_loop(0, BODY // 8, boxes, (blank,) * (BOXES - 1))
-        pltpu.make_async_copy(ded.at[b], ded_hbm.at[b], out_sem.at[b, 0]).start()
-        pltpu.make_async_copy(peak.at[b], peak_hbm.at[b], out_sem.at[b, 1]).start()
+            rows = slice(half * 8, half * 8 + 8)
+            running = [top[pl.ds(half * 8 * BODY + c, 8, stride=BODY), :] for c in range(BODY)]
+            for c in range(BODY):
+                ded[b, rows, c * LANES : (c + 1) * LANES] = running[c]
+            best = running
+            for k in range(BOXES - 1):
+                width = 2**k
+                late = [blank] + running[:-1]
+                if width < LANES:
+                    late = [
+                        pltpu.roll(jnp.where(one_lane < LANES - width, now, old), width, 1)
+                        for now, old in zip(running, late)
+                    ]
+                running = [now + old for now, old in zip(running, late)]
+                scale = 1.0 / math.sqrt(2 * width)
+                best = [jnp.maximum(high, now * scale) for high, now in zip(best, running)]
+            for c in range(BODY):
+                peak[b, rows, c * LANES : (c + 1) * LANES] = best[c]
         return 0
 
     lax.fori_loop(0, BEAMS, step_three, 0)
 
     def finish(b, _):
-        pltpu.make_async_copy(ded.at[b], ded_hbm.at[b], out_sem.at[b, 0]).wait()
-        pltpu.make_async_copy(peak.at[b], peak_hbm.at[b], out_sem.at[b, 1]).wait()
         for k in range(len(peers1)):
             send_one(b, k).wait_send()
         for k in range(len(peers2)):
@@ -322,9 +344,11 @@
     return pl.pallas_call(
         kernel,
         out_shape=(plane, plane),
-        in_specs=[pl.BlockSpec(memory_space=pltpu.SMEM), pl.BlockSpec(memory_space=pl.ANY)],
-        out_specs=(pl.BlockSpec(memory_space=pl.ANY), pl.BlockSpec(memory_space=pl.ANY)),
+        in_specs=[pl.BlockSpec(memory_space=pltpu.VMEM), pl.BlockSpec(memory_space=pl.ANY)],
+        out_specs=(pl.BlockSpec(memory_space=pltpu.VMEM), pl.BlockSpec(memory_space=pltpu.VMEM)),
         scratch_shapes=[
+            pltpu.VMEM((8, LANES), jnp.int32),
+            pltpu.SMEM((8, LANES), jnp.int32),
             pltpu.VMEM((BEAMS, 128, 8192), jnp.bfloat16),
             vmem(8 * PITCH, LANES),
             vmem(16 * PITCH, LANES),
@@ -339,10 +363,8 @@
             vmem(16 * PITCH, LANES),
             vmem(16 * TOP_PITCH, LANES),
             vmem(16 * BODY, LANES),
-            vmem(BEAMS, ROWS, 8192),
-            vmem(BEAMS, ROWS, 8192),
+            dma,
             dma((BEAMS,)),
-            dma((BEAMS, 2)),
             dma((BEAMS, 7)),
             dma((BEAMS, 8)),
             dma((BEAMS,)),
@@ -353,7 +375,7 @@
         compiler_params=pltpu.CompilerParams(
             collective_id=0, has_side_effects=True, vmem_limit_bytes=48 * 2**20
         ),
-    )(shift_table(channel_spans), intensity)
+    )(channel_spans.reshape(128, LANES), intensity)
 
 
 def solution(mesh):

time: 98.8 us -> 64.6 us (0.65)
  Pallas kernels: 80.1 us -> 60.4 us
  other arithmetic: 6.46 us -> 0 us
  between operations: 4.77 us -> 0.65 us
  local copies, waits for them, and re-layouts: 7.25 us -> 3.47 us
    pallas_call x1, Pallas kernels: 80.1 us -> 60.4 us  [on_device(): pl.pallas_call(kernel, out_shape=(plane, plane), in_specs=[pl.BlockSpec(m...]
    reshape x16 -> x0, local copies, waits for them, and re-layouts: 2.27 us -> none  [the longest x1 1.02 us: shift_table(): sums = spans.reshape(1024, 16).sum(axis=1)]
    reshape x2 -> x0, other arithmetic: 2.11 us -> none  [shift_table(): tables.append((r * low // (low + high)).reshape(-1))]
    slice x3 -> x0, local copies, waits for them, and re-layouts: 1.77 us -> none  [shift_table(): low, high = (grouped[:, 0:1], grouped[:, 1:2])]
    slice x6 -> x0, other arithmetic: 1.38 us -> none  [shift_table(): low, high = (grouped[:, 0:1], grouped[:, 1:2])]
    reduce_sum x10 -> x0, other arithmetic: 1.36 us -> none  [the longest x8 1.05 us: shift_table(): grouped = widths.reshape(16 // rows, 2, -1).sum(axis=2)]
    select_n x7 -> x0, other arithmetic: 1.19 us -> none  [shift_table(): tables.append((r * low // (low + high)).reshape(-1))]
    unnamed x2 -> x4, local copies, waits for them, and re-layouts: 2.64 us -> 3.47 us
where the time goes in v1:
time: 64.6 us; the launch traced here: 64.5 us
  Pallas kernels  60.4 us (93%)
  local copies, waits for them, and re-layouts  3.47 us (5%)
  between operations  0.65 us (1%)
    pallas_call x1, Pallas kernels, on_device(): pl.pallas_call(kernel, out_shape=(plane, plane), in_specs=[pl.BlockSpec(m...  60.4 us
    unnamed x4, local copies, waits for them, and re-layouts  3.47 us

profile of v1, /device:TPU:1, one launch (start us, length us, event | category | flops | bytes accessed | tf_op | source)
XLA Modules:
  0.0 64.5 jit_solution(6211331921396625523)
XLA Ops:
  0.6 0.0 copy-start
  0.6 0.8 %copy-done = s32[16384]{0:T(1024)S(1)} copy-done((s32[16384]{0:T(1024)S(1)}, s32[16384]{0:T(1024)}, u32[]{:S(2)}) %copy-start) | copy-done | bytes 65560
  1.5 60.4 %shard_map.41 = (f32[4,16,8192]{2,1,0:T(8,128)S(1)}, f32[4,16,8192]{2,1,0:T(8,128)S(1)}) custom-call(s32[128,128]{1,0:T(8,128)S(1)} %bitcast.1, bf16[4,128,8192]{2,1,0:T(8,128)(2,1)} %x_hbm.1), custom_call_target="tpu_custom_call" | custom-call | tf_op jit(solution)/shard_map/pallas_call | solution.py:344
  61.8 1.3 %copy.6 = f32[4,16,8192]{2,1,0:T(8,128)} copy(f32[4,16,8192]{2,1,0:T(8,128)S(1)} %get-tuple-element.4) | data formatting | bytes 4194304
  63.2 1.3 %copy.7 = f32[4,16,8192]{2,1,0:T(8,128)} copy(f32[4,16,8192]{2,1,0:T(8,128)S(1)} %get-tuple-element.5) | data formatting | bytes 4194304
Async XLA Ops:
  0.6 0.8 %copy-start = (s32[16384]{0:T(1024)S(1)}, s32[16384]{0:T(1024)}, u32[]{:S(2)}) copy-start(s32[16384]{0:T(1024)} %param.3) | copy-start | bytes 196612

commit v2 on v1

--- a/solution.py
+++ b/solution.py
@@ -10,6 +10,7 @@
 ROWS = 16
 BOXES = 9
 BEAMS = 4
+LAST = BEAMS - 1
 LANES = 128
 BODY = 64
 PAD = 8
@@ -72,10 +73,34 @@
     out[1:2, :] = jnp.sum(jnp.where(diagonal, shifts, 0.0), axis=0, keepdims=True).astype(jnp.int32)
 
 
+def boxcar(top, ded, peak, b, halves=(0, 1)):
+    one_lane = lax.broadcasted_iota(jnp.int32, (8, LANES), 1)
+    blank = jnp.zeros((8, LANES), jnp.float32)
+    for half in halves:
+        rows = slice(half * 8, half * 8 + 8)
+        running = [top[pl.ds(half * 8 * BODY + c, 8, stride=BODY), :] for c in range(BODY)]
+        for c in range(BODY):
+            ded[b, rows, c * LANES : (c + 1) * LANES] = running[c]
+        best = running
+        for k in range(BOXES - 1):
+            width = 2**k
+            late = [blank] + running[:-1]
+            if width < LANES:
+                late = [
+                    pltpu.roll(jnp.where(one_lane < LANES - width, now, old), width, 1)
+                    for now, old in zip(running, late)
+                ]
+            running = [now + old for now, old in zip(running, late)]
+            scale = 1.0 / math.sqrt(2 * width)
+            best = [jnp.maximum(high, now * scale) for high, now in zip(best, running)]
+        for c in range(BODY):
+            peak[b, rows, c * LANES : (c + 1) * LANES] = best[c]
+
+
 def kernel(
-    spans, x_hbm, ded, peak,
-    shifts, table, xbuf, g, t5, t6, p7, r1, t8, t9, p10, r2, t11, t12, t13, top,
-    table_sem, in_sem, send1, recv1, own1, send2, recv2, own2,
+    spans_hbm, x_hbm, ded, peak, top,
+    shifts, table, xbuf, g, t5, t6, p7, r1, t8, t9, p10, r2, t11, t12, t13, spans,
+    spans_sem, table_sem, in_sem, send1, recv1, own1, send2, recv2, own2,
 ):
     sub, band = lax.axis_index("sub"), lax.axis_index("band")
     y, z, x_lo = sub // 8, sub // 2 % 4, sub % 2
@@ -107,26 +132,20 @@
     def fetch(b):
         return pltpu.make_async_copy(x_hbm.at[b], xbuf.at[b], in_sem.at[b])
 
-    for b in range(BEAMS):
-        fetch(b).start()
+    fetch_spans = pltpu.make_async_copy(spans_hbm, spans, spans_sem)
+    fetch_spans.start()
+    fetch(0).start()
 
     zeros = jnp.zeros((PAD, LANES), jnp.float32)
-    for ref, count in ((g, 8), (t5, 16), (t6, 16), (t8, 16), (t9, 16), (t11, 16), (t12, 16)):
-        for row in range(count):
-            ref[pl.ds(row * PITCH, PAD), :] = zeros
-    for row in range(16):
-        t13[pl.ds(row * TOP_PITCH, PAD), :] = zeros
-        t13[pl.ds(row * TOP_PITCH + PAD, PAD), :] = zeros
-
-    def clear(b, _):
-        for row in range(16):
-            r1[b, row // 2, row % 2, 0:PAD, :] = zeros
-            r2[b, row, 0:PAD, :] = zeros
-        return 0
-
-    lax.fori_loop(0, BEAMS, clear, 0)
+    def clear_rows(*filled):
+        for ref, count in filled:
+            for row in range(count):
+                ref[pl.ds(row * PITCH, PAD), :] = zeros
+
+    clear_rows((g, 8), (t5, 16), (t6, 16))
 
     block = rev3(j)
+    fetch_spans.wait()
     fill_tables(
         spans, shifts, band * 32 + sub, band * 32 + y * 8, block, block * 16 + rev2(y) * 4 + rev2(band)
     )
@@ -209,8 +228,6 @@
         )
 
     def first(b):
-        fetch(b).wait()
-
         for c in range(8192 // COLUMNS):
             part = jnp.dot(
                 ones, xbuf[b, :, c * COLUMNS : (c + 1) * COLUMNS], preferred_element_type=jnp.float32
@@ -232,11 +249,28 @@
             send_one(b, k).start()
         keep_one(b).start()
 
+    fetch(0).wait()
+    for b in range(1, BEAMS):
+        fetch(b).start()
     first(0)
     pl.semaphore_wait(barrier, len(peers1) + len(peers2))
     start_one(0)
 
+    clear_rows((t8, 16), (t9, 16), (t11, 16), (t12, 16))
+    for row in range(16):
+        t13[pl.ds(row * TOP_PITCH, PAD), :] = zeros
+        t13[pl.ds(row * TOP_PITCH + PAD, PAD), :] = zeros
+
+    def clear(b, _):
+        for row in range(16):
+            r1[b, row // 2, row % 2, 0:PAD, :] = zeros
+            r2[b, row, 0:PAD, :] = zeros
+        return 0
+
+    lax.fori_loop(0, BEAMS, clear, 0)
+
     def step_one(b, _):
+        fetch(b).wait()
         first(b)
         start_one(b)
         return 0
@@ -266,8 +300,6 @@
         return 0
 
     lax.fori_loop(0, BEAMS, step_two, 0)
-
-    one_lane = lax.broadcasted_iota(jnp.int32, (8, LANES), 1)
 
     def step_three(b, _):
         keep_two(b).wait()
@@ -303,26 +335,11 @@
 
         large_level(14, 16, load13, store14)
 
-        blank = jnp.zeros((8, LANES), jnp.float32)
-        for half in range(2):
-            rows = slice(half * 8, half * 8 + 8)
-            running = [top[pl.ds(half * 8 * BODY + c, 8, stride=BODY), :] for c in range(BODY)]
-            for c in range(BODY):
-                ded[b, rows, c * LANES : (c + 1) * LANES] = running[c]
-            best = running
-            for k in range(BOXES - 1):
-                width = 2**k
-                late = [blank] + running[:-1]
-                if width < LANES:
-                    late = [
-                        pltpu.roll(jnp.where(one_lane < LANES - width, now, old), width, 1)
-                        for now, old in zip(running, late)
-                    ]
-                running = [now + old for now, old in zip(running, late)]
-                scale = 1.0 / math.sqrt(2 * width)
-                best = [jnp.maximum(high, now * scale) for high, now in zip(best, running)]
-            for c in range(BODY):
-                peak[b, rows, c * LANES : (c + 1) * LANES] = best[c]
+
+        @pl.when(b < LAST)
+        def _():
+            boxcar(top, ded, peak, b)
+
         return 0
 
     lax.fori_loop(0, BEAMS, step_three, 0)
@@ -337,15 +354,35 @@
     lax.fori_loop(0, BEAMS, finish, 0)
 
 
+def writer(ded_done, peak_done, top, ded, peak, ded_last, peak_last, sem, last_sem):
+    copies = []
+    for k, (done, out) in enumerate(((ded_done, ded), (peak_done, peak))):
+        for b in range(LAST):
+            copies.append(pltpu.make_async_copy(done.at[b], out.at[b], sem.at[k, b]))
+    for copy in copies:
+        copy.start()
+    for half in range(2):
+        boxcar(top, ded_last, peak_last, 0, (half,))
+        rows = pl.ds(8 * half, 8)
+        for k, (made, out) in enumerate(((ded_last, ded), (peak_last, peak))):
+            copies.append(pltpu.make_async_copy(made.at[0, rows], out.at[LAST, rows], last_sem.at[k, half]))
+            copies[-1].start()
+    for copy in copies:
+        copy.wait()
+
+
 def on_device(intensity, channel_spans):
+    done = jax.ShapeDtypeStruct((LAST, ROWS, 8192), jnp.float32)
     plane = jax.ShapeDtypeStruct((BEAMS, ROWS, 8192), jnp.float32)
     vmem = lambda *shape: pltpu.VMEM(shape, jnp.float32)
     dma = pltpu.SemaphoreType.DMA
-    return pl.pallas_call(
+    in_vmem = pl.BlockSpec(memory_space=pltpu.VMEM)
+    anywhere = pl.BlockSpec(memory_space=pl.ANY)
+    ded_done, peak_done, top = pl.pallas_call(
         kernel,
-        out_shape=(plane, plane),
-        in_specs=[pl.BlockSpec(memory_space=pltpu.VMEM), pl.BlockSpec(memory_space=pl.ANY)],
-        out_specs=(pl.BlockSpec(memory_space=pltpu.VMEM), pl.BlockSpec(memory_space=pltpu.VMEM)),
+        out_shape=(done, done, jax.ShapeDtypeStruct((16 * BODY, LANES), jnp.float32)),
+        in_specs=[anywhere, anywhere],
+        out_specs=(in_vmem, in_vmem, in_vmem),
         scratch_shapes=[
             pltpu.VMEM((8, LANES), jnp.int32),
             pltpu.SMEM((8, LANES), jnp.int32),
@@ -362,7 +399,8 @@
             vmem(16 * PITCH, LANES),
             vmem(16 * PITCH, LANES),
             vmem(16 * TOP_PITCH, LANES),
-            vmem(16 * BODY, LANES),
+            pltpu.VMEM((128, LANES), jnp.int32),
+            dma,
             dma,
             dma((BEAMS,)),
             dma((BEAMS, 7)),
@@ -376,6 +414,14 @@
             collective_id=0, has_side_effects=True, vmem_limit_bytes=48 * 2**20
         ),
     )(channel_spans.reshape(128, LANES), intensity)
+    return pl.pallas_call(
+        writer,
+        out_shape=(plane, plane),
+        in_specs=[in_vmem] * 3,
+        out_specs=(anywhere, anywhere),
+        scratch_shapes=[vmem(1, ROWS, 8192), vmem(1, ROWS, 8192), dma((2, LAST)), dma((2, 2))],
+        compiler_params=pltpu.CompilerParams(vmem_limit_bytes=16 * 2**20),
+    )(ded_done, peak_done, top)
 
 
 def solution(mesh):

time: 64.6 us -> 63.9 us (0.989)
  local copies, waits for them, and re-layouts: 3.47 us -> 0.83 us
  Pallas kernels: 60.4 us -> 62.3 us
    unnamed x4 -> x2, local copies, waits for them, and re-layouts: 3.47 us -> 0.83 us
    pallas_call x1 -> x2, Pallas kernels: 60.4 us -> 62.3 us  [the longest x1 59.3 us: on_device(): pl.pallas_call(kernel, out_shape=(done, done, jax.ShapeDtypeStruct((16 *...]
where the time goes in v2:
time: 63.9 us; the launch traced here: 63.8 us
  Pallas kernels  62.3 us (97%)
  local copies, waits for them, and re-layouts  0.83 us (1%)
  between operations  0.65 us (1%)
    pallas_call x1, Pallas kernels, on_device(): pl.pallas_call(kernel, out_shape=(done, done, jax.ShapeDtypeStruct((16 *...  59.3 us
    pallas_call x1, Pallas kernels, on_device(): pl.pallas_call(writer, out_shape=(plane, plane), in_specs=[in_vmem] * 3,...  3.02 us

profile of v2, /device:TPU:1, one launch (start us, length us, event | category | flops | bytes accessed | tf_op | source)
XLA Modules:
  0.0 63.8 jit_solution(8331573013461456424)
XLA Ops:
  0.6 0.0 copy-start
  0.6 0.8 %copy-done = s32[16384]{0:T(1024)S(1)} copy-done((s32[16384]{0:T(1024)S(1)}, s32[16384]{0:T(1024)}, u32[]{:S(2)}) %copy-start) | copy-done | bytes 65560
  1.5 59.3 %shard_map.41 = (f32[3,16,8192]{2,1,0:T(8,128)S(1)}, f32[3,16,8192]{2,1,0:T(8,128)S(1)}, f32[1024,128]{1,0:T(8,128)S(1)}) custom-call(s32[128,128]{1,0:T(8,128)S(1)} %bitcast.1, bf16[4,128,8192]{2,1,0:T(8,128)(2,1)} %x_hbm.1), custom_call_target="tpu_custom_call" | custom-call | tf_op jit(solution)/shard_map/pallas_call | solution.py:381
  60.7 3.0 %shard_map.42 = (f32[4,16,8192]{2,1,0:T(8,128)}, f32[4,16,8192]{2,1,0:T(8,128)}) custom-call(f32[3,16,8192]{2,1,0:T(8,128)S(1)} %get-tuple-element.5.ded_done, f32[3,16,8192]{2,1,0:T(8,128)S(1)} %get-tuple-element.6.peak_done, f32[1024,128]{1,0:T(8,128)S(1)} %get-tuple-element.7.top), custom_call_target="tpu_custom_call" | custom-call | tf_op jit(solution)/shard_map/pallas_call | solution.py:417
Async XLA Ops:
  0.6 0.8 %copy-start = (s32[16384]{0:T(1024)S(1)}, s32[16384]{0:T(1024)}, u32[]{:S(2)}) copy-start(s32[16384]{0:T(1024)} %param.3) | copy-start | bytes 196612

commit v3 on v2

--- a/solution.py
+++ b/solution.py
@@ -18,6 +18,10 @@
 TOP_PAD = 16
 TOP_PITCH = TOP_PAD + BODY
 COLUMNS = 1024
+SHARED = 1
+ALONE = BEAMS - SHARED
+ORDER = (3, 0, 1, 2)
+PLACE = (0, 1, 3, 2)
 
 
 def rev2(v):
@@ -41,23 +45,33 @@
     return jnp.where(left < 0, guess - 1, jnp.where(left >= bottom, guess + 1, guess))
 
 
-def fill_tables(spans, out, device, group, block, own):
+def fill_tables(spans, out, device, group, near_block, own, pair_block, blocks, turn):
     spread = spans[...].astype(jnp.float32)
     totals = jnp.sum(spread, axis=1, keepdims=True)
+    devices = lax.broadcasted_iota(jnp.int32, (128, LANES), 0)
     entry = lax.broadcasted_iota(jnp.int32, (1, LANES), 1)
+
+    def shifts_of(r, start, half):
+        place = devices - start
+        low = jnp.sum(jnp.where((place >= 0) & (place < half), totals, 0.0), axis=0, keepdims=True)
+        both = jnp.sum(jnp.where((place >= 0) & (place < 2 * half), totals, 0.0), axis=0, keepdims=True)
+        return quotient(r * low.astype(jnp.int32), jnp.maximum(both.astype(jnp.int32), 1))
+
     level = entry // 16
     near = level < 3
     rows = jnp.where(near, powers(level, 4), powers(level - 3, 2))
     half = powers(level, 1)
     start = jnp.where(near, group, 0) + entry % 16 // rows * 2 * half
-    r = rows * jnp.where(near, block, own) + entry % 16 % rows
-    place = lax.broadcasted_iota(jnp.int32, (128, LANES), 0) - start
-    low = jnp.sum(jnp.where((place >= 0) & (place < half), totals, 0.0), axis=0, keepdims=True)
-    both = jnp.sum(jnp.where((place >= 0) & (place < 2 * half), totals, 0.0), axis=0, keepdims=True)
-    low, both = low.astype(jnp.int32), jnp.maximum(both.astype(jnp.int32), 1)
-    out[0:1, :] = quotient(r * low, both)
-
-    mine = spans[pl.ds(device, 1), :].astype(jnp.float32)
+    out[0:1, :] = shifts_of(rows * jnp.where(near, near_block, own) + entry % 16 % rows, start, half)
+
+    eight, nine = entry < 32, entry < 64
+    kept = (entry + turn) % 2
+    row9 = 8 * jnp.where(entry % 32 // 16 == 0, blocks[0], blocks[1]) + entry % 8
+    row10 = 16 * jnp.where(kept == 0, blocks[0], blocks[1]) + entry % 16
+    r = jnp.where(eight, entry, jnp.where(nine, row9, row10))
+    start = jnp.where(eight, pair_block, group + jnp.where(nine, entry % 16 // 8 * 4, 0))
+    out[3:4, :] = shifts_of(r, start, jnp.where(eight, 1, jnp.where(nine, 2, 4)))
+
     entry = lax.broadcasted_iota(jnp.int32, (48, 1), 0)
     level = entry // 16
     rows = powers(level, 4)
@@ -65,12 +79,14 @@
     start = entry % 16 // rows * 2 * half
     r = entry % 16 % rows
     place = lax.broadcasted_iota(jnp.int32, (48, LANES), 1) - start
-    low = jnp.sum(jnp.where((place >= 0) & (place < half), mine, 0.0), axis=1, keepdims=True)
-    both = jnp.sum(jnp.where((place >= 0) & (place < 2 * half), mine, 0.0), axis=1, keepdims=True)
-    low, both = low.astype(jnp.int32), jnp.maximum(both.astype(jnp.int32), 1)
-    shifts = quotient(r * low, both).astype(jnp.float32)
     diagonal = entry == lax.broadcasted_iota(jnp.int32, (48, LANES), 1)
-    out[1:2, :] = jnp.sum(jnp.where(diagonal, shifts, 0.0), axis=0, keepdims=True).astype(jnp.int32)
+    for at, which in ((1, device), (2, 2 * pair_block + 1 - device)):
+        mine = spans[pl.ds(which, 1), :].astype(jnp.float32)
+        low = jnp.sum(jnp.where((place >= 0) & (place < half), mine, 0.0), axis=1, keepdims=True)
+        both = jnp.sum(jnp.where((place >= 0) & (place < 2 * half), mine, 0.0), axis=1, keepdims=True)
+        low, both = low.astype(jnp.int32), jnp.maximum(both.astype(jnp.int32), 1)
+        shifts = quotient(r * low, both).astype(jnp.float32)
+        out[at : at + 1, :] = jnp.sum(jnp.where(diagonal, shifts, 0.0), axis=0, keepdims=True).astype(jnp.int32)
 
 
 def boxcar(top, ded, peak, b, halves=(0, 1)):
@@ -98,9 +114,10 @@
 
 
 def kernel(
-    spans_hbm, x_hbm, ded, peak, top,
-    shifts, table, xbuf, g, t5, t6, p7, r1, t8, t9, p10, r2, t11, t12, t13, spans,
-    spans_sem, table_sem, in_sem, send1, recv1, own1, send2, recv2, own2,
+    spans, x_hbm, ded, peak, top,
+    shifts, table, xbuf, g, t5, t6, p7, r1, t8, t9, p10, r2, t11, t12, t13,
+    rg, q7, q8, rz, t9q,
+    table_sem, in_sem, send1, recv1, own1, send2, recv2, own2, send_x, recv_x, send_z, recv_z, own_z,
 ):
     sub, band = lax.axis_index("sub"), lax.axis_index("band")
     y, z, x_lo = sub // 8, sub // 2 % 4, sub % 2
@@ -108,13 +125,18 @@
     j = sub % 8
     m = band * 4 + y
 
-    peers1 = []
+    peers1, peers_z = [], []
     for dz in (0, 1, 3, 2):
         for dx in range(2):
+            z_to = (z + dz) % 4
+            to = z_to * 2 + (x_lo + dx) % 2
+            device = {"sub": y * 8 + to, "band": band}
             if dz or dx:
-                to = (z + dz) % 4 * 2 + (x_lo + dx) % 2
-                peers1.append((to, {"sub": y * 8 + to, "band": band}))
-    peers2 = []
+                peers1.append((to, device))
+            if dz and not dx:
+                peers_z.append((z_to, device))
+    x_partner = peers1[0][1]
+    peers2, peers3 = [], []
     for dy in (0, 1, 3, 2):
         for dh in range(2):
             for dc in range(2):
@@ -122,39 +144,65 @@
                     y_to = (y + dy) % 4
                     band_to = (x_hi + dh) % 2 * 2 + (core + dc) % 2
                     peers2.append((y_to, band_to, {"sub": y_to * 8 + j, "band": band_to}))
+                    other = y_to * 8 + z * 2 + (x_lo + dh) % 2
+                    peers3.append((y_to, band_to, {"sub": other, "band": band_to}, dh))
 
     barrier = pltpu.get_barrier_semaphore()
-    for peer in peers1:
-        pl.semaphore_signal(barrier, inc=1, device_id=peer[-1], device_id_type=pl.DeviceIdType.MESH)
-    for peer in peers2:
-        pl.semaphore_signal(barrier, inc=1, device_id=peer[-1], device_id_type=pl.DeviceIdType.MESH)
+    greeted = [p[1] for p in peers1] + [p[2] for p in peers2] + [p[2] for p in peers3 if p[3]]
+    for peer in greeted:
+        pl.semaphore_signal(barrier, inc=1, device_id=peer, device_id_type=pl.DeviceIdType.MESH)
 
     def fetch(b):
-        return pltpu.make_async_copy(x_hbm.at[b], xbuf.at[b], in_sem.at[b])
-
-    fetch_spans = pltpu.make_async_copy(spans_hbm, spans, spans_sem)
-    fetch_spans.start()
-    fetch(0).start()
+        return pltpu.make_async_copy(x_hbm.at[PLACE[b]], xbuf.at[b], in_sem.at[b])
+
+    for b in ORDER:
+        fetch(b).start()
 
     zeros = jnp.zeros((PAD, LANES), jnp.float32)
-    def clear_rows(*filled):
-        for ref, count in filled:
-            for row in range(count):
-                ref[pl.ds(row * PITCH, PAD), :] = zeros
-
-    clear_rows((g, 8), (t5, 16), (t6, 16))
+    for ref, count in ((t5, 16), (t6, 16), (t8, 16), (t9, 16), (t11, 16), (t12, 16), (t9q, 32)):
+        for row in range(count):
+            ref[pl.ds(row * PITCH, PAD), :] = zeros
+    for row in range(16):
+        t13[pl.ds(row * TOP_PITCH, PAD), :] = zeros
+        t13[pl.ds(row * TOP_PITCH + PAD, PAD), :] = zeros
+
+    def clear(b, _):
+        for row in range(16):
+            r2[b, row, 0:PAD, :] = zeros
+        return 0
+
+    lax.fori_loop(0, BEAMS, clear, 0)
+
+    def clear_alone(t, _):
+        for row in range(16):
+            r1[t, row // 2, row % 2, 0:PAD, :] = zeros
+        return 0
+
+    lax.fori_loop(0, ALONE, clear_alone, 0)
+
+    def clear_shared(t, _):
+        for row in range(16):
+            q7[t, 0, row, 0:PAD, :] = zeros
+            q7[t, 1, row, 0:PAD, :] = zeros
+        for row in range(32):
+            rz[t, row // 8, row // 4 % 2, row % 4, 0:PAD, :] = zeros
+        return 0
+
+    lax.fori_loop(0, SHARED, clear_shared, 0)
 
     block = rev3(j)
-    fetch_spans.wait()
+    turn = x_lo + x_hi
+    device = band * 32 + sub
     fill_tables(
-        spans, shifts, band * 32 + sub, band * 32 + y * 8, block, block * 16 + rev2(y) * 4 + rev2(band)
+        spans, shifts, device, band * 32 + y * 8, block, block * 16 + rev2(y) * 4 + rev2(band),
+        device // 2 * 2, (rev2(z), 4 + rev2(z)), turn,
     )
     to_scalar = pltpu.make_async_copy(shifts, table, table_sem)
     to_scalar.start()
     to_scalar.wait()
 
-    def shift_of(level, entry):
-        return table[0, (level - 8) * 16 + entry] if level >= 8 else table[1, (level - 5) * 16 + entry]
+    def shift_of(level, entry, at=1):
+        return table[0, (level - 8) * 16 + entry] if level >= 8 else table[at, (level - 5) * 16 + entry]
 
     lane = lax.broadcasted_iota(jnp.int32, (BODY, LANES), 1)
 
@@ -171,7 +219,15 @@
             ref[pl.ds(row * PITCH + PAD, BODY), :] = value
         return store
 
-    def small_level(level, rows, load, store, single=False):
+    top_row = lax.broadcasted_iota(jnp.int32, (BODY, LANES), 0) == 0
+
+    def sums_of(ref, at):
+        def load(row, back):
+            value = ref[at, pl.ds(row * BODY - back, BODY), :]
+            return jnp.where(top_row, 0.0, value) if back else value
+        return load
+
+    def small_level(level, rows, load, store, single=False, at=1):
         for entry in range(16):
             pair, i = entry // rows, entry % rows
             if single:
@@ -179,7 +235,7 @@
             else:
                 low = pair * rows + i // 2
                 high = low + rows // 2
-            amount = shift_of(level, entry)
+            amount = shift_of(level, entry, at)
             store(entry, load(low, 0) + moved(load(high, 0), load(high, 1), amount))
 
     def large_level(level, rows, load, store):
@@ -227,63 +283,125 @@
             p10.at[b, rev2(y) * 4 + rev2(band)], r2.at[b, m, pl.ds(PAD, BODY), :], own2.at[b]
         )
 
-    def first(b):
+    def send_three(b, k):
+        y_to, band_to, device, _ = peers3[k]
+        return pltpu.make_async_remote_copy(
+            src_ref=p10.at[b, rev2(y_to) * 4 + rev2(band_to)],
+            dst_ref=r2.at[b, m, pl.ds(PAD, BODY), :],
+            send_sem=send2.at[b, k],
+            recv_sem=recv2.at[b, m],
+            device_id=device,
+            device_id_type=pl.DeviceIdType.MESH,
+        )
+
+    def share(t):
+        return pltpu.make_async_remote_copy(
+            src_ref=g.at[t + ALONE],
+            dst_ref=rg.at[t],
+            send_sem=send_x.at[t],
+            recv_sem=recv_x.at[t],
+            device_id=x_partner,
+            device_id_type=pl.DeviceIdType.MESH,
+        )
+
+    def send_rows(t, k):
+        z_to, device = peers_z[k]
+        return pltpu.make_async_remote_copy(
+            src_ref=q8.at[t, :, pl.ds(4 * rev2(z_to), 4)],
+            dst_ref=rz.at[t, z, :, :, pl.ds(PAD, BODY), :],
+            send_sem=send_z.at[t, k],
+            recv_sem=recv_z.at[t, z],
+            device_id=device,
+            device_id_type=pl.DeviceIdType.MESH,
+        )
+
+    def keep_rows(t):
+        return pltpu.make_async_copy(
+            q8.at[t, :, pl.ds(4 * rev2(z), 4)], rz.at[t, z, :, :, pl.ds(PAD, BODY), :], own_z.at[t]
+        )
+
+    def channel_sums(b):
+        fetch(b).wait()
         for c in range(8192 // COLUMNS):
             part = jnp.dot(
                 ones, xbuf[b, :, c * COLUMNS : (c + 1) * COLUMNS], preferred_element_type=jnp.float32
             )
             for k in range(COLUMNS // LANES):
-                g[pl.ds(PAD + c * (COLUMNS // LANES) + k, 8, stride=PITCH), :] = part[
+                g[b, pl.ds(c * (COLUMNS // LANES) + k, 8, stride=BODY), :] = part[
                     0:8, k * LANES : (k + 1) * LANES
                 ]
-        small_level(5, 4, flat(g), flat_store(t5), single=True)
-        small_level(6, 8, flat(t5), flat_store(t6))
-
+
+    def device_rows(load, store, at=1):
+        small_level(5, 4, load, flat_store(t5), single=True, at=at)
+        small_level(6, 8, flat(t5), flat_store(t6), at=at)
+        small_level(7, 16, flat(t6), store, at=at)
+
+    def start_one(b):
         def keep(row, value):
             p7[b, row] = value
 
-        small_level(7, 16, flat(t6), keep)
-
-    def start_one(b):
-        for k in range(len(peers1)):
+        device_rows(sums_of(g, b), keep)
+        if b < 2:
+            for k in straight:
+                send_one(b, k).start()
+        keep_one(b).start()
+
+    straight, crossing = (1, 3, 5), (0, 2, 4, 6)
+
+    def start_crossing(b):
+        for k in crossing if b < 2 else crossing + straight:
             send_one(b, k).start()
-        keep_one(b).start()
-
-    fetch(0).wait()
-    for b in range(1, BEAMS):
-        fetch(b).start()
-    first(0)
-    pl.semaphore_wait(barrier, len(peers1) + len(peers2))
+
+    def pair_rows(t, x, load, at):
+        def keep(row, value):
+            q7[t, x, row, PAD : PAD + BODY, :] = value
+
+        device_rows(load, keep, at)
+
+    channel_sums(3)
+    pl.semaphore_wait(barrier, len(greeted))
+    share(0).start()
+    channel_sums(0)
     start_one(0)
-
-    clear_rows((t8, 16), (t9, 16), (t11, 16), (t12, 16))
-    for row in range(16):
-        t13[pl.ds(row * TOP_PITCH, PAD), :] = zeros
-        t13[pl.ds(row * TOP_PITCH + PAD, PAD), :] = zeros
-
-    def clear(b, _):
-        for row in range(16):
-            r1[b, row // 2, row % 2, 0:PAD, :] = zeros
-            r2[b, row, 0:PAD, :] = zeros
-        return 0
-
-    lax.fori_loop(0, BEAMS, clear, 0)
-
-    def step_one(b, _):
-        fetch(b).wait()
-        first(b)
+    start_crossing(0)
+    pair_rows(0, x_lo, sums_of(g, 3), 1)
+    for b in (1, 2):
+        channel_sums(b)
         start_one(b)
-        return 0
-
-    lax.fori_loop(1, BEAMS, step_one, 0)
-
-    def step_two(b, _):
+
+    def send_pair_rows(t):
+        for k in range(len(peers_z)):
+            send_rows(t, k).start()
+        keep_rows(t).start()
+
+    def step_pair(t):
+        pair_rows(t, 1 - x_lo, sums_of(rg, t), 2)
+        for r in range(32):
+            near = q7[t, 1, r // 2, PAD : PAD + BODY, :]
+            far = q7[t, 1, r // 2, PAD - 1 : PAD - 1 + BODY, :]
+            q8[t, r // 16, r % 16] = q7[t, 0, r // 2, PAD : PAD + BODY, :] + moved(near, far, table[3, r])
+
+    share(0).wait_recv()
+    start_crossing(1)
+    step_pair(0)
+    send_pair_rows(0)
+
+    def wait_ring(t):
+        keep_rows(t).wait()
+        for z_to, _ in peers_z:
+            pltpu.make_async_copy(
+                rz.at[t, z_to, :, :, pl.ds(PAD, BODY), :], rz.at[t, z_to, :, :, pl.ds(PAD, BODY), :],
+                recv_z.at[t, z_to],
+            ).wait()
+
+    def wait_one(b):
         keep_one(b).wait()
         for to, _ in peers1:
             pltpu.make_async_copy(
                 r1.at[b, to, :, pl.ds(PAD, BODY), :], r1.at[b, to, :, pl.ds(PAD, BODY), :], recv1.at[b, to]
             ).wait()
 
+    def step_two(b):
         def load(row, back):
             return r1[b, row // 2, row % 2, PAD - back : PAD - back + BODY, :]
 
@@ -297,11 +415,28 @@
         for k in range(len(peers2)):
             send_two(b, k).start()
         keep_two(b).start()
-        return 0
-
-    lax.fori_loop(0, BEAMS, step_two, 0)
-
-    def step_three(b, _):
+
+    def step_ring(t):
+        for entry in range(32):
+            side, pair, i = entry // 16, entry // 8 % 2, entry % 8
+            near = rz[t, 2 * pair + 1, side, i // 2, PAD : PAD + BODY, :]
+            far = rz[t, 2 * pair + 1, side, i // 2, PAD - 1 : PAD - 1 + BODY, :]
+            t9q[pl.ds(entry * PITCH + PAD, BODY), :] = rz[
+                t, 2 * pair, side, i // 2, PAD : PAD + BODY, :
+            ] + moved(near, far, table[3, 32 + entry])
+        for row in range(16):
+            low = (turn + row) % 2 * 16 + row // 2
+
+            def load(at, back):
+                start = pl.multiple_of(at * PITCH, 8) + (PAD - back)
+                return t9q[pl.ds(start, BODY), :]
+
+            p10[t + ALONE, row] = load(low, 0) + moved(load(low + 8, 0), load(low + 8, 1), table[3, 64 + row])
+        for k in range(len(peers3)):
+            send_three(t + ALONE, k).start()
+        keep_two(t + ALONE).start()
+
+    def step_three(b):
         keep_two(b).wait()
         for y_to, band_to, _ in peers2:
             n = band_to * 4 + y_to
@@ -335,23 +470,41 @@
 
         large_level(14, 16, load13, store14)
 
-
-        @pl.when(b < LAST)
-        def _():
-            boxcar(top, ded, peak, b)
-
+        if PLACE[b] < LAST:
+            boxcar(top, ded, peak, PLACE[b])
+
+    wait_one(0)
+    step_two(0)
+    wait_one(1)
+    start_crossing(2)
+    step_two(1)
+    wait_ring(0)
+    step_ring(0)
+    wait_one(2)
+    step_two(2)
+    step_three(0)
+    step_three(1)
+    step_three(3)
+    step_three(2)
+
+    def finish_alone(t, _):
+        for k in range(len(peers1)):
+            send_one(t, k).wait_send()
+        for k in range(len(peers2)):
+            send_two(t, k).wait_send()
         return 0
 
-    lax.fori_loop(0, BEAMS, step_three, 0)
-
-    def finish(b, _):
-        for k in range(len(peers1)):
-            send_one(b, k).wait_send()
-        for k in range(len(peers2)):
-            send_two(b, k).wait_send()
+    lax.fori_loop(0, ALONE, finish_alone, 0)
+
+    def finish_shared(t, _):
+        share(t).wait_send()
+        for k in range(len(peers_z)):
+            send_rows(t, k).wait_send()
+        for k in range(len(peers3)):
+            send_three(t + ALONE, k).wait_send()
         return 0
 
-    lax.fori_loop(0, BEAMS, finish, 0)
+    lax.fori_loop(0, SHARED, finish_shared, 0)
 
 
 def writer(ded_done, peak_done, top, ded, peak, ded_last, peak_last, sem, last_sem):
@@ -381,17 +534,17 @@
     ded_done, peak_done, top = pl.pallas_call(
         kernel,
         out_shape=(done, done, jax.ShapeDtypeStruct((16 * BODY, LANES), jnp.float32)),
-        in_specs=[anywhere, anywhere],
+        in_specs=[in_vmem, anywhere],
         out_specs=(in_vmem, in_vmem, in_vmem),
         scratch_shapes=[
             pltpu.VMEM((8, LANES), jnp.int32),
             pltpu.SMEM((8, LANES), jnp.int32),
             pltpu.VMEM((BEAMS, 128, 8192), jnp.bfloat16),
-            vmem(8 * PITCH, LANES),
+            vmem(BEAMS, 8 * BODY, LANES),
             vmem(16 * PITCH, LANES),
             vmem(16 * PITCH, LANES),
-            vmem(BEAMS, 16, BODY, LANES),
-            vmem(BEAMS, 8, 2, PITCH, LANES),
+            vmem(ALONE, 16, BODY, LANES),
+            vmem(ALONE, 8, 2, PITCH, LANES),
             vmem(16 * PITCH, LANES),
             vmem(16 * PITCH, LANES),
             vmem(BEAMS, 16, BODY, LANES),
@@ -399,16 +552,24 @@
             vmem(16 * PITCH, LANES),
             vmem(16 * PITCH, LANES),
             vmem(16 * TOP_PITCH, LANES),
-            pltpu.VMEM((128, LANES), jnp.int32),
-            dma,
+            vmem(SHARED, 8 * BODY, LANES),
+            vmem(SHARED, 2, 16, PITCH, LANES),
+            vmem(SHARED, 2, 16, BODY, LANES),
+            vmem(SHARED, 4, 2, 4, PITCH, LANES),
+            vmem(32 * PITCH, LANES),
             dma,
             dma((BEAMS,)),
-            dma((BEAMS, 7)),
-            dma((BEAMS, 8)),
-            dma((BEAMS,)),
+            dma((ALONE, 7)),
+            dma((ALONE, 8)),
+            dma((ALONE,)),
             dma((BEAMS, 15)),
             dma((BEAMS, 16)),
             dma((BEAMS,)),
+            dma((SHARED,)),
+            dma((SHARED,)),
+            dma((SHARED, 3)),
+            dma((SHARED, 4)),
+            dma((SHARED,)),
         ],
         compiler_params=pltpu.CompilerParams(
             collective_id=0, has_side_effects=True, vmem_limit_bytes=48 * 2**20

time: 63.9 us -> 63.3 us (level)
  Pallas kernels: 62.3 us -> 61.5 us
    pallas_call x1, Pallas kernels: 59.3 us -> 58.4 us  [on_device(): pl.pallas_call(kernel, out_shape=(done, done, jax.ShapeDtypeStruct((16 *...]
where the time goes in v3:
time: 63.3 us; the launch traced here: 63.1 us
  Pallas kernels  61.5 us (97%)
  local copies, waits for them, and re-layouts  0.83 us (1%)
  between operations  0.81 us (1%)
    pallas_call x1, Pallas kernels, on_device(): pl.pallas_call(kernel, out_shape=(done, done, jax.ShapeDtypeStruct((16 *...  58.4 us
    pallas_call x1, Pallas kernels, on_device(): pl.pallas_call(writer, out_shape=(plane, plane), in_specs=[in_vmem] * 3,...  3.02 us

profile of v3, /device:TPU:1, one launch (start us, length us, event | category | flops | bytes accessed | tf_op | source)
XLA Modules:
  0.0 63.1 jit_solution(11346285354354516605)
XLA Ops:
  0.6 0.0 copy-start
  0.6 0.8 %copy-done = s32[16384]{0:T(1024)S(1)} copy-done((s32[16384]{0:T(1024)S(1)}, s32[16384]{0:T(1024)}, u32[]{:S(2)}) %copy-start) | copy-done | bytes 65560
  1.5 58.4 %shard_map.41 = (f32[3,16,8192]{2,1,0:T(8,128)S(1)}, f32[3,16,8192]{2,1,0:T(8,128)S(1)}, f32[1024,128]{1,0:T(8,128)S(1)}) custom-call(s32[128,128]{1,0:T(8,128)S(1)} %bitcast.1, bf16[4,128,8192]{2,1,0:T(8,128)(2,1)} %x_hbm.1), custom_call_target="tpu_custom_call" | custom-call | tf_op jit(solution)/shard_map/pallas_call | solution.py:534
  59.9 3.0 %shard_map.42 = (f32[4,16,8192]{2,1,0:T(8,128)}, f32[4,16,8192]{2,1,0:T(8,128)}) custom-call(f32[3,16,8192]{2,1,0:T(8,128)S(1)} %get-tuple-element.5.ded_done, f32[3,16,8192]{2,1,0:T(8,128)S(1)} %get-tuple-element.6.peak_done, f32[1024,128]{1,0:T(8,128)S(1)} %get-tuple-element.7.top), custom_call_target="tpu_custom_call" | custom-call | tf_op jit(solution)/shard_map/pallas_call | solution.py:578
Async XLA Ops:
  0.6 0.8 %copy-start = (s32[16384]{0:T(1024)S(1)}, s32[16384]{0:T(1024)}, u32[]{:S(2)}) copy-start(s32[16384]{0:T(1024)} %param.3) | copy-start | bytes 196612

commit v4 on v3

--- a/solution.py
+++ b/solution.py
@@ -155,40 +155,12 @@
     def fetch(b):
         return pltpu.make_async_copy(x_hbm.at[PLACE[b]], xbuf.at[b], in_sem.at[b])
 
-    for b in ORDER:
-        fetch(b).start()
+    fetch(ORDER[0]).start()
 
     zeros = jnp.zeros((PAD, LANES), jnp.float32)
-    for ref, count in ((t5, 16), (t6, 16), (t8, 16), (t9, 16), (t11, 16), (t12, 16), (t9q, 32)):
-        for row in range(count):
-            ref[pl.ds(row * PITCH, PAD), :] = zeros
     for row in range(16):
-        t13[pl.ds(row * TOP_PITCH, PAD), :] = zeros
-        t13[pl.ds(row * TOP_PITCH + PAD, PAD), :] = zeros
-
-    def clear(b, _):
-        for row in range(16):
-            r2[b, row, 0:PAD, :] = zeros
-        return 0
-
-    lax.fori_loop(0, BEAMS, clear, 0)
-
-    def clear_alone(t, _):
-        for row in range(16):
-            r1[t, row // 2, row % 2, 0:PAD, :] = zeros
-        return 0
-
-    lax.fori_loop(0, ALONE, clear_alone, 0)
-
-    def clear_shared(t, _):
-        for row in range(16):
-            q7[t, 0, row, 0:PAD, :] = zeros
-            q7[t, 1, row, 0:PAD, :] = zeros
-        for row in range(32):
-            rz[t, row // 8, row // 4 % 2, row % 4, 0:PAD, :] = zeros
-        return 0
-
-    lax.fori_loop(0, SHARED, clear_shared, 0)
+        t5[pl.ds(row * PITCH, PAD), :] = zeros
+        t6[pl.ds(row * PITCH, PAD), :] = zeros
 
     block = rev3(j)
     turn = x_lo + x_hi
@@ -322,6 +294,9 @@
 
     def channel_sums(b):
         fetch(b).wait()
+        if b == ORDER[0]:
+            for later in ORDER[1:]:
+                fetch(later).start()
         for c in range(8192 // COLUMNS):
             part = jnp.dot(
                 ones, xbuf[b, :, c * COLUMNS : (c + 1) * COLUMNS], preferred_element_type=jnp.float32
@@ -364,6 +339,36 @@
     channel_sums(0)
     start_one(0)
     start_crossing(0)
+    for ref, count in ((t8, 16), (t9, 16), (t11, 16), (t12, 16), (t9q, 32)):
+        for row in range(count):
+            ref[pl.ds(row * PITCH, PAD), :] = zeros
+    for row in range(16):
+        t13[pl.ds(row * TOP_PITCH, PAD), :] = zeros
+        t13[pl.ds(row * TOP_PITCH + PAD, PAD), :] = zeros
+
+    def clear(b, _):
+        for row in range(16):
+            r2[b, row, 0:PAD, :] = zeros
+        return 0
+
+    lax.fori_loop(0, BEAMS, clear, 0)
+
+    def clear_alone(t, _):
+        for row in range(16):
+            r1[t, row // 2, row % 2, 0:PAD, :] = zeros
+        return 0
+
+    lax.fori_loop(0, ALONE, clear_alone, 0)
+
+    def clear_shared(t, _):
+        for row in range(16):
+            q7[t, 0, row, 0:PAD, :] = zeros
+            q7[t, 1, row, 0:PAD, :] = zeros
+        for row in range(32):
+            rz[t, row // 8, row // 4 % 2, row % 4, 0:PAD, :] = zeros
+        return 0
+
+    lax.fori_loop(0, SHARED, clear_shared, 0)
     pair_rows(0, x_lo, sums_of(g, 3), 1)
     for b in (1, 2):
         channel_sums(b)

time: 63.3 us -> 65.1 us (1.028)
  Pallas kernels: 61.5 us -> 63.4 us
    pallas_call x1, Pallas kernels: 58.4 us -> 60.4 us  [on_device(): pl.pallas_call(kernel, out_shape=(done, done, jax.ShapeDtypeStruct((16 *...]
where the time goes in v4:
time: 65.1 us; the launch traced here: 64.9 us
  Pallas kernels  63.4 us (97%)
  local copies, waits for them, and re-layouts  0.83 us (1%)
    pallas_call x1, Pallas kernels, on_device(): pl.pallas_call(kernel, out_shape=(done, done, jax.ShapeDtypeStruct((16 *...  60.4 us
    pallas_call x1, Pallas kernels, on_device(): pl.pallas_call(writer, out_shape=(plane, plane), in_specs=[in_vmem] * 3,...  3.02 us

profile of v4, /device:TPU:1, one launch (start us, length us, event | category | flops | bytes accessed | tf_op | source)
XLA Modules:
  0.0 64.9 jit_solution(17018721550799538883)
XLA Ops:
  0.6 0.0 copy-start
  0.6 0.8 %copy-done = s32[16384]{0:T(1024)S(1)} copy-done((s32[16384]{0:T(1024)S(1)}, s32[16384]{0:T(1024)}, u32[]{:S(2)}) %copy-start) | copy-done | bytes 65560
  1.5 60.4 %shard_map.41 = (f32[3,16,8192]{2,1,0:T(8,128)S(1)}, f32[3,16,8192]{2,1,0:T(8,128)S(1)}, f32[1024,128]{1,0:T(8,128)S(1)}) custom-call(s32[128,128]{1,0:T(8,128)S(1)} %bitcast.1, bf16[4,128,8192]{2,1,0:T(8,128)(2,1)} %x_hbm.1), custom_call_target="tpu_custom_call" | custom-call | tf_op jit(solution)/shard_map/pallas_call | solution.py:539
  61.9 3.0 %shard_map.42 = (f32[4,16,8192]{2,1,0:T(8,128)}, f32[4,16,8192]{2,1,0:T(8,128)}) custom-call(f32[3,16,8192]{2,1,0:T(8,128)S(1)} %get-tuple-element.5.ded_done, f32[3,16,8192]{2,1,0:T(8,128)S(1)} %get-tuple-element.6.peak_done, f32[1024,128]{1,0:T(8,128)S(1)} %get-tuple-element.7.top), custom_call_target="tpu_custom_call" | custom-call | tf_op jit(solution)/shard_map/pallas_call | solution.py:583
Async XLA Ops:
  0.6 0.8 %copy-start = (s32[16384]{0:T(1024)S(1)}, s32[16384]{0:T(1024)}, u32[]{:S(2)}) copy-start(s32[16384]{0:T(1024)} %param.3) | copy-start | bytes 196612
